TPU v7x, 256 devices: a whole 4x4x8 slice. The times are simulated.
256 devices in a mesh: con: 16 (over z_hi, x, core), res: 16 (over y, z_lo).
Axes of the slice: x: 4, y: 4, z: 8 (z_hi: 2, z_lo: 4; z = z_hi * 4 + z_lo), core: 2. Of those that a mesh axis runs over, the one named last changes fastest.
Arguments:
- integrals: float32 [24576, 24576], P('res', 'con'), as said below
- tile_mask: int32 [96, 96], P('res', 'con'), may hold values from 0 to 1, as said below
- amplitudes: float32 [24576, 384], P(('con', 'res')), may hold values from -4 to 4
- other_first: float32 [24576, 384], P(('res', 'con')), may hold values from -6 to 6
- other_second: float32 [24576, 384], P(('con', 'res')), may hold values from -6 to 6
- vir_index: int32 [2, 24576], replicated, may hold values from 0 to 1599
- occ_index: int32 [2, 384], replicated, may hold values from 0 to 31, as said below
- partner: int32 [384], replicated, may hold values from 0 to 383, as said below
- eps_vir: float32 [1600], replicated, may hold values from 0.2 to 3
- eps_occ: float32 [32], replicated, may hold values from -2 to -0.2
Outputs:
- first_update: float32 [24576, 384], P(('res', 'con'))
- second_update: float32 [24576, 384], P(('con', 'res'))
Inputs may be any that keep to these rules, and one draw needn't show every extreme that they name: integrals is symmetric: integrals[p, s] == integrals[s, p]. tile_mask is symmetric and its diagonal is 1. partner is a permutation that is its own inverse with no fixed point. The two orbitals of an occupied pair differ, and occ_index[0, partner[q]] == occ_index[1, q].
All inputs are finite; a program needn't handle non-finite values.
Results may differ from a plain program's by a relative error of at most 0.000065.
Values sent between devices are 32-bit elements; how exact they have to be, the bound alone decides.
A program may use at most 128 MiB of HBM per device.

v0:
```python
import jax
import jax.numpy as jnp
from jax import lax
from jax.sharding import PartitionSpec as P

W = 256
precise = lax.Precision.HIGHEST


def pair_energy(pair_index, table):
    orbitals = lax.broadcasted_iota(jnp.int32, (1, table.shape[0]), 1)
    counts = (pair_index[0][:, None] == orbitals).astype(jnp.float32) + (
        pair_index[1][:, None] == orbitals
    ).astype(jnp.float32)
    return jnp.dot(counts, table, precision=precise, preferred_element_type=jnp.float32)


def vir_energy_rows(vir_index, eps_vir, row_offset, row_count):
    picked = lax.dynamic_slice_in_dim(vir_index, row_offset, row_count, 1)
    block_rows = min(row_count, 512)
    blocks = picked.reshape(2, row_count // block_rows, block_rows).transpose(1, 0, 2)
    energies = lax.map(lambda part_index: pair_energy(part_index, eps_vir), blocks)
    return energies.reshape(row_count)


def renew(ladder, other, vir_rows, occ_energy, swap_matrix):
    unscaled = (other + ladder) / (vir_rows[:, None] - occ_energy[None, :])
    swapped = jnp.dot(unscaled, swap_matrix, precision=precise, preferred_element_type=jnp.float32)
    return 0.5 * (unscaled - swapped)


def per_device(
    integrals,
    tile_mask,
    amplitudes,
    other_first,
    other_second,
    vir_index,
    occ_index,
    partner,
    eps_vir,
    eps_occ,
):
    row_count, col_count = integrals.shape
    tiles_down, tiles_across = tile_mask.shape
    weights = tile_mask.astype(jnp.float32)
    screened = (
        integrals.reshape(tiles_down, W, tiles_across, W) * weights[:, None, :, None]
    ).reshape(row_count, col_count)
    occ_energy = pair_energy(occ_index, eps_occ)
    occ_cols = amplitudes.shape[1]
    column_ids = lax.broadcasted_iota(jnp.int32, (occ_cols, occ_cols), 0)
    swap_matrix = (column_ids == partner[None, :]).astype(jnp.float32)
    n_con = lax.axis_size("con")
    n_res = lax.axis_size("res")
    con_at = lax.axis_index("con")
    res_at = lax.axis_index("res")
    fine_rows = amplitudes.shape[0]
    partial_one = jnp.dot(
        screened,
        lax.all_gather(amplitudes, "res", axis=0, tiled=True),
        precision=precise,
        preferred_element_type=jnp.float32,
    )
    ladder_one = lax.psum_scatter(partial_one, "con", scatter_dimension=0, tiled=True)
    first_offset = (res_at * n_con + con_at) * fine_rows
    first_vir = vir_energy_rows(vir_index, eps_vir, first_offset, fine_rows)
    first_update = renew(ladder_one, other_first, first_vir, occ_energy, swap_matrix)
    partial_two = lax.dot_general(
        screened,
        lax.all_gather(first_update, "con", axis=0, tiled=True),
        (((0,), (0,)), ((), ())),
        precision=precise,
        preferred_element_type=jnp.float32,
    )
    ladder_two = lax.psum_scatter(partial_two, "res", scatter_dimension=0, tiled=True)
    second_offset = (con_at * n_res + res_at) * fine_rows
    second_vir = vir_energy_rows(vir_index, eps_vir, second_offset, fine_rows)
    second_update = renew(ladder_two, other_second, second_vir, occ_energy, swap_matrix)
    return (first_update, second_update)


def solution(mesh):
    return jax.shard_map(
        per_device,
        mesh=mesh,
        in_specs=(
            P("res", "con"),
            P("res", "con"),
            P(("con", "res"), None),
            P(("res", "con"), None),
            P(("con", "res"), None),
            P(),
            P(),
            P(),
            P(),
            P(),
        ),
        out_specs=(P(("res", "con"), None), P(("con", "res"), None)),
        check_vma=False,
    )
```

profile of v0, /device:TPU:2, one launch (start us, length us, event | category | flops | bytes accessed | tf_op | source)
XLA Modules:
  0.0 389.8 jit_solution(10868963700371033135)
XLA Ops:
  7.2 0.0 copy-start
  7.2 0.0 all-gather.3.cloned.1.call-start
  7.2 0.7 all-gather.3.cloned.1.call-update
  7.9 0.0 reduce-scatter.3.cloned.1.call-start
  8.0 0.7 convert_element_type.26
  8.7 0.9 mul.29
  9.5 8.4 %copy.12 = f32[192,8,6,256]{3,1,2,0:T(8,128)} copy(f32[192,8,6,256]{3,2,1,0:T(8,128)S(1)} %bitcast.24) | data formatting | bytes 18874368
  17.9 12.2 %mul.31 = f32[1536,1536]{1,0:T(8,128)} multiply(f32[1536,1536]{1,0:T(8,128)} %param.10, f32[1536,1536]{1,0:T(8,128)} %bitcast.25) | non-fusion elementwise | flops 2359296 | bytes 28311552 | tf_op jit(solution)/shard_map/mul | solution.py:48
  30.1 71.9 %all-gather.3.cloned.1.call-done = f32[1536,384]{1,0:T(8,128)} async-done(((f32[96,384]{1,0:T(8,128)}), f32[1536,384]{1,0:T(8,128)}) %all-gather.3.cloned.1.call-update) | async-done | bytes 2359312 | tf_op jit(solution)/shard_map/all_gather | solution.py:61
  101.9 18.8 %fusion.30 = f32[1536,384]{1,0:T(8,128)} fusion(f32[1536,1536]{1,0:T(8,128)} %mul.31, f32[1536,384]{1,0:T(8,128)} %all-gather.3.cloned.1.call-done), kind=kOutput, calls=%fused_computation.50 | convolution fusion | flops 10871635968 | bytes 14155776 | tf_op jit(solution)/shard_map/dot_general | solution.py:59
  120.8 0.0 copy-start.5
  120.8 0.0 reduce-scatter.3.cloned.1.call-update
  120.8 0.2 all-gather.5.cloned.1.call-start
  121.1 0.4 copy-done.1
  121.5 0.8 constant_dynamic-slice_fusion
  122.2 0.0 copy-done.2
  122.3 0.0 copy-done
  122.3 0.5 convolution_reduce_fusion
  122.8 0.8 convolution_bitcast_fusion.1
  123.6 84.8 %reduce-scatter.3.cloned.1.call-done = f32[96,384]{1,0:T(8,128)} async-done(((f32[1536,384]{1,0:T(8,128)}), f32[96,384]{1,0:T(8,128)}) %reduce-scatter.3.cloned.1.call-update) | async-done | bytes 147472 | tf_op jit(solution)/shard_map/reduce_scatter | solution.py:65
  208.4 0.0 copy-done.3
  208.4 0.0 copy-done.5
  208.4 2.0 fusion
  210.4 0.0 all-gather.5.cloned.1.call-update
  210.4 0.0 reduce-scatter.5.cloned.1.call-start
  210.4 62.1 %all-gather.5.cloned.1.call-done = f32[1536,384]{1,0:T(8,128)} async-done(((f32[96,384]{1,0:T(8,128)}), f32[1536,384]{1,0:T(8,128)}) %all-gather.5.cloned.1.call-update) | async-done | bytes 2359312 | tf_op jit(solution)/shard_map/all_gather | solution.py:71
  272.5 19.1 %fusion.31 = f32[1536,384]{1,0:T(8,128)} fusion(f32[1536,1536]{1,0:T(8,128)} %mul.31, f32[1536,384]{1,0:T(8,128)} %all-gather.5.cloned.1.call-done), kind=kOutput, calls=%fused_computation.51 | convolution fusion | flops 10871635968 | bytes 14155776 | tf_op jit(solution)/shard_map/dot_general | solution.py:69
  291.6 0.0 reduce-scatter.5.cloned.1.call-update
  291.7 0.8 convolution_bitcast_fusion
  292.5 88.8 %reduce-scatter.5.cloned.1.call-done = f32[96,384]{1,0:T(8,128)} async-done(((f32[1536,384]{1,0:T(8,128)}), f32[96,384]{1,0:T(8,128)}) %reduce-scatter.5.cloned.1.call-update) | async-done | bytes 147472 | tf_op jit(solution)/shard_map/reduce_scatter | solution.py:76
  381.3 0.0 copy-done.4
  381.3 2.0 fusion.1
  (7 shorter events, 0.0 us)
Async XLA Ops:
  7.2 115.1 %copy-start = (f32[32]{0:T(128)S(1)}, f32[32]{0:T(128)}, u32[]{:S(2)}) copy-start(f32[32]{0:T(128)} %param.19) | copy-start | bytes 388
  7.2 94.8 %all-gather.3.cloned.1.call-start = ((), (), s32[]{:S(2)}) async-start(), calls=%async_computation.2 | async-start | bytes 2506752 | tf_op jit(solution)/shard_map/all_gather | solution.py:61
  7.9 200.5 %reduce-scatter.3.cloned.1.call-start = ((), (), s32[]{:S(2)}) async-start(), calls=%async_computation.3 | async-start | bytes 2506752 | tf_op jit(solution)/shard_map/reduce_scatter | solution.py:65
  120.8 0.7 copy-start.1
  120.8 1.5 copy-start.2
  120.8 87.6 %copy-start.3 = (f32[96,384]{1,0:T(8,128)S(1)}, f32[96,384]{1,0:T(8,128)}, u32[]{:S(2)}) copy-start(f32[96,384]{1,0:T(8,128)} %param.13) | copy-start | bytes 442372
  120.8 87.6 %copy-start.5 = (s32[384]{0:T(512)S(1)}, s32[384]{0:T(512)}, u32[]{:S(2)}) copy-start(s32[384]{0:T(512)} %param.17) | copy-start | bytes 4612
  120.8 151.7 %all-gather.5.cloned.1.call-start = ((), (), s32[]{:S(2)}) async-start(), calls=%async_computation.4 | async-start | bytes 2506752 | tf_op jit(solution)/shard_map/all_gather | solution.py:71
  210.4 170.9 %reduce-scatter.5.cloned.1.call-start = ((), (), s32[]{:S(2)}) async-start(), calls=%async_computation.5 | async-start | bytes 2506752 | tf_op jit(solution)/shard_map/reduce_scatter | solution.py:76
  291.6 89.7 %copy-start.4 = (f32[96,384]{1,0:T(8,128)S(1)}, f32[96,384]{1,0:T(8,128)}, u32[]{:S(2)}) copy-start(f32[96,384]{1,0:T(8,128)} %param.14) | copy-start | bytes 442372
Sparse Core Ops, SparseCore 0:
  9.8 92.0 all-gather.2
  120.9 87.3 reduce-scatter.2
  211.7 60.7 all-gather.4
  291.8 89.4 reduce-scatter.4
where the time goes:
time: 390 us
  waiting for transfers between devices  308 us (79%)
  matrix products  44 us (11%)
  between operations  13.8 us (4%)
  other arithmetic  12.9 us (3%)
  local copies, waits for them, and re-layouts  10.5 us (3%)
    reduce_scatter x1, waiting for transfers between devices, per_device(): lax.psum_scatter(partial_two, 'res', scatter_dimension=0, tiled=True)  88.8 us
    reduce_scatter x1, waiting for transfers between devices, per_device(): lax.psum_scatter(partial_one, 'con', scatter_dimension=0, tiled=True)  84.8 us
    all_gather x1, waiting for transfers between devices, per_device(): lax.all_gather(amplitudes, 'res', axis=0, tiled=True)  71.9 us
    all_gather x1, waiting for transfers between devices, per_device(): lax.all_gather(first_update, 'con', axis=0, tiled=True)  62.1 us
    dot_general x1, matrix products, per_device(): lax.dot_general(screened, lax.all_gather(first_update, 'con', axis=0, til...  19.1 us
    dot_general x1, matrix products, per_device(): jnp.dot(screened, lax.all_gather(amplitudes, 'res', axis=0, tiled=True),...  18.8 us
    mul x1, other arithmetic, per_device(): integrals.reshape(tiles_down, W, tiles_across, W)  12.2 us
    unnamed x14, local copies, waits for them, and re-layouts  8.81 us
  transfers between devices with their start and end apart: 4, of which 4 were waited for; matrix products, arithmetic and copies ran while one was open for 6% of the time, Pallas kernels for 0%

commit v1 on v0

--- a/solution.py
+++ b/solution.py
@@ -58,7 +58,9 @@
     fine_rows = amplitudes.shape[0]
     partial_one = jnp.dot(
         screened,
-        lax.all_gather(amplitudes, "res", axis=0, tiled=True),
+        jnp.concatenate(
+            lax.all_to_all(jnp.stack([amplitudes] * lax.axis_size("res")), "res", 0, 0), axis=0
+        ),
         precision=precise,
         preferred_element_type=jnp.float32,
     )

time: 390 us -> 363 us (0.931)
  waiting for transfers between devices: 308 us -> 270 us
  starting transfers between devices: 0.34 us -> 9.12 us
    all_gather x1 -> x0, waiting for transfers between devices: 71.9 us -> none  [per_device(): lax.all_gather(amplitudes, 'res', axis=0, tiled=True)]
    all_to_all x0 -> x1, waiting for transfers between devices: none -> 34.5 us  [per_device(): lax.all_to_all(jnp.stack([amplitudes] * lax.axis_size('res')), 'res', 0, 0)]
    all_to_all x0 -> x1, starting transfers between devices: none -> 8.81 us  [per_device(): lax.all_to_all(jnp.stack([amplitudes] * lax.axis_size('res')), 'res', 0, 0)]
    unnamed x14 -> x16, local copies, waits for them, and re-layouts: 8.81 us -> 8.81 us
  transfers between devices with their start and end apart: 4 -> 4, of which waited for: 4 -> 4; matrix products, arithmetic and copies ran while one was open for 6% -> 7% of each run, Pallas kernels for 0% -> 0%
where the time goes in v1:
time: 363 us
  waiting for transfers between devices  270 us (74%)
  matrix products  44 us (12%)
  between operations  13.8 us (4%)
  local copies, waits for them, and re-layouts  13.1 us (4%)
  other arithmetic  12.2 us (3%)
  starting transfers between devices  9.12 us (3%)
    reduce_scatter x1, waiting for transfers between devices, per_device(): lax.psum_scatter(partial_two, 'res', scatter_dimension=0, tiled=True)  88.4 us
    reduce_scatter x1, waiting for transfers between devices, per_device(): lax.psum_scatter(partial_one, 'con', scatter_dimension=0, tiled=True)  85.3 us
    all_gather x1, waiting for transfers between devices, per_device(): lax.all_gather(first_update, 'con', axis=0, tiled=True)  62 us
    all_to_all x1, waiting for transfers between devices, per_device(): lax.all_to_all(jnp.stack([amplitudes] * lax.axis_size('res')), 'res', 0, 0)  34.5 us
    dot_general x1, matrix products, per_device(): lax.dot_general(screened, lax.all_gather(first_update, 'con', axis=0, til...  19.1 us
    dot_general x1, matrix products, per_device(): jnp.dot(screened, jnp.concatenate(lax.all_to_all(jnp.stack([amplitudes] *...  18.8 us
    mul x1, other arithmetic, per_device(): integrals.reshape(tiles_down, W, tiles_across, W)  12.2 us
    all_to_all x1, starting transfers between devices, per_device(): lax.all_to_all(jnp.stack([amplitudes] * lax.axis_size('res')), 'res', 0, 0)  8.81 us
  transfers between devices with their start and end apart: 4, of which 4 were waited for; matrix products, arithmetic and copies ran while one was open for 7% of the time, Pallas kernels for 0%

profile of v1, /device:TPU:2, one launch (start us, length us, event | category | flops | bytes accessed | tf_op | source)
XLA Modules:
  0.0 362.6 jit_solution(10224527469894926557)
XLA Ops:
  7.2 0.0 copy-start
  7.2 2.6 stack.2
  9.8 8.8 %all-to-all-start = ((f32[16,96,384]{2,1,0:T(8,128)}), f32[16,96,384]{2,1,0:T(8,128)}, u32[]{:S(2)}, u32[]{:S(2)}) async-start(f32[16,96,384]{2,1,0:T(8,128)} %stack.2), calls=%async_computation | async-start | bytes 4718592 | tf_op jit(solution)/shard_map/all_to_all | solution.py:62
  18.6 0.0 reduce-scatter.3.cloned.1.call-start
  18.7 0.0 copy-done.2
  18.7 0.9 mul.29
  19.6 8.4 %copy.12 = f32[192,8,6,256]{3,1,2,0:T(8,128)} copy(f32[192,8,6,256]{3,2,1,0:T(8,128)S(1)} %bitcast.25) | data formatting | bytes 18874368
  27.9 12.2 %mul.31 = f32[1536,1536]{1,0:T(8,128)} multiply(f32[1536,1536]{1,0:T(8,128)} %param.10, f32[1536,1536]{1,0:T(8,128)} %bitcast.26) | non-fusion elementwise | flops 2359296 | bytes 28311552 | tf_op jit(solution)/shard_map/mul | solution.py:48
  40.1 34.5 %all-to-all-done = f32[16,96,384]{2,1,0:T(8,128)} async-done(((f32[16,96,384]{2,1,0:T(8,128)}), f32[16,96,384]{2,1,0:T(8,128)}, u32[]{:S(2)}, u32[]{:S(2)}) %all-to-all-start) | async-done | bytes 2359328 | tf_op jit(solution)/shard_map/all_to_all | solution.py:62
  74.6 18.8 %fusion.30 = f32[1536,384]{1,0:T(8,128)} fusion(f32[1536,1536]{1,0:T(8,128)} %mul.31, f32[1536,384]{1,0:T(8,128)} %bitcast), kind=kOutput, calls=%fused_computation.50 | convolution fusion | flops 10871635968 | bytes 14155776 | tf_op jit(solution)/shard_map/dot_general | solution.py:59
  93.5 0.0 copy-start.6
  93.5 0.0 reduce-scatter.3.cloned.1.call-update
  93.5 0.2 all-gather.2.cloned.1.call-start
  93.7 0.4 copy-done.1
  94.2 0.8 constant_dynamic-slice_fusion
  94.9 0.0 copy-done.3
  94.9 0.0 copy-done
  95.0 0.5 convolution_reduce_fusion
  95.4 0.8 convolution_bitcast_fusion.1
  96.2 85.3 %reduce-scatter.3.cloned.1.call-done = f32[96,384]{1,0:T(8,128)} async-done(((f32[1536,384]{1,0:T(8,128)}), f32[96,384]{1,0:T(8,128)}) %reduce-scatter.3.cloned.1.call-update) | async-done | bytes 147472 | tf_op jit(solution)/shard_map/reduce_scatter | solution.py:67
  181.6 0.0 copy-done.4
  181.6 0.0 copy-done.6
  181.6 2.0 fusion
  183.6 0.0 all-gather.2.cloned.1.call-update
  183.6 0.0 reduce-scatter.5.cloned.1.call-start
  183.6 62.0 %all-gather.2.cloned.1.call-done = f32[1536,384]{1,0:T(8,128)} async-done(((f32[96,384]{1,0:T(8,128)}), f32[1536,384]{1,0:T(8,128)}) %all-gather.2.cloned.1.call-update) | async-done | bytes 2359312 | tf_op jit(solution)/shard_map/all_gather | solution.py:73
  245.7 19.1 %fusion.31 = f32[1536,384]{1,0:T(8,128)} fusion(f32[1536,1536]{1,0:T(8,128)} %mul.31, f32[1536,384]{1,0:T(8,128)} %all-gather.2.cloned.1.call-done), kind=kOutput, calls=%fused_computation.51 | convolution fusion | flops 10871635968 | bytes 14155776 | tf_op jit(solution)/shard_map/dot_general | solution.py:71
  264.8 0.0 reduce-scatter.5.cloned.1.call-update
  264.8 0.8 convolution_bitcast_fusion
  265.6 88.4 %reduce-scatter.5.cloned.1.call-done = f32[96,384]{1,0:T(8,128)} async-done(((f32[1536,384]{1,0:T(8,128)}), f32[96,384]{1,0:T(8,128)}) %reduce-scatter.5.cloned.1.call-update) | async-done | bytes 147472 | tf_op jit(solution)/shard_map/reduce_scatter | solution.py:78
  354.1 0.0 copy-done.5
  354.1 2.0 fusion.1
  (9 shorter events, 0.0 us)
Async XLA Ops:
  7.2 87.8 %copy-start = (f32[32]{0:T(128)S(1)}, f32[32]{0:T(128)}, u32[]{:S(2)}) copy-start(f32[32]{0:T(128)} %param.19) | copy-start | bytes 388
  9.8 8.9 %copy-start.2 = (s32[6,6]{1,0:T(8,128)S(1)}, s32[6,6]{1,0:T(8,128)}, u32[]{:S(2)}) copy-start(s32[6,6]{1,0:T(8,128)} %param.11) | copy-start | bytes 436
  9.8 64.8 %all-to-all-start = ((f32[16,96,384]{2,1,0:T(8,128)}), f32[16,96,384]{2,1,0:T(8,128)}, u32[]{:S(2)}, u32[]{:S(2)}) async-start(f32[16,96,384]{2,1,0:T(8,128)} %stack.2), calls=%async_computation | async-start | bytes 4718592 | tf_op jit(solution)/shard_map/all_to_all | solution.py:62
  18.6 163.0 %reduce-scatter.3.cloned.1.call-start = ((), (), s32[]{:S(2)}) async-start(), calls=%async_computation.3 | async-start | bytes 2506752 | tf_op jit(solution)/shard_map/reduce_scatter | solution.py:67
  93.5 0.7 copy-start.1
  93.5 1.5 copy-start.3
  93.5 88.1 %copy-start.4 = (f32[96,384]{1,0:T(8,128)S(1)}, f32[96,384]{1,0:T(8,128)}, u32[]{:S(2)}) copy-start(f32[96,384]{1,0:T(8,128)} %param.13) | copy-start | bytes 442372
  93.5 88.1 %copy-start.6 = (s32[384]{0:T(512)S(1)}, s32[384]{0:T(512)}, u32[]{:S(2)}) copy-start(s32[384]{0:T(512)} %param.17) | copy-start | bytes 4612
  93.5 152.2 %all-gather.2.cloned.1.call-start = ((), (), s32[]{:S(2)}) async-start(), calls=%async_computation.4 | async-start | bytes 2506752 | tf_op jit(solution)/shard_map/all_gather | solution.py:73
  183.6 170.5 %reduce-scatter.5.cloned.1.call-start = ((), (), s32[]{:S(2)}) async-start(), calls=%async_computation.5 | async-start | bytes 2506752 | tf_op jit(solution)/shard_map/reduce_scatter | solution.py:78
  264.8 89.3 %copy-start.5 = (f32[96,384]{1,0:T(8,128)S(1)}, f32[96,384]{1,0:T(8,128)}, u32[]{:S(2)}) copy-start(f32[96,384]{1,0:T(8,128)} %param.14) | copy-start | bytes 442372
Sparse Core Ops, SparseCore 0:
  93.6 87.9 reduce-scatter.2
  184.9 60.7 all-gather.1
  265.0 89.0 reduce-scatter.4
